TPU v7x, 32 devices: a whole 2x2x4 slice. The times are simulated.
32 devices in a mesh: region: 4 (over z), dev: 8 (over y, x, core).
Axes of the slice: x: 2, y: 2, z: 4, core: 2. Of those that a mesh axis runs over, the one named last changes fastest.
Arguments:
- loads: float32 [256, 32, 1024], P(('region', 'dev')), may hold values from -50 to 50
- factor: bfloat16 [256, 1024, 1024], P(('region', 'dev')), may hold values from -1 to 1, as said below
- pivots: float32 [256, 1024], P(('region', 'dev')), may hold values from 0.04 to 0.14, as said below
- lower: float32 [256, 1024], P(('region', 'dev')), may hold values from -1 to -0.2
- upper: float32 [256, 1024], P(('region', 'dev')), may hold values from 0.2 to 1
- incidence: int32 [256, 16], P(('region', 'dev')), may hold values from 0 to 511, as said below
- counts: int32 [256], P(('region', 'dev')), may hold values from 8 to 16, as said below
Outputs:
- dispatch: float32 [256, 32, 1024], P(('region', 'dev'))
- duals: float32 [256, 16, 128], P(('region', 'dev'))
- residuals: float32 [14, 2], replicated
Inputs may be any that keep to these rules, and one draw needn't show every extreme that they name: `incidence`: slot j of area a is live when j < counts[a]. Bus b is owned by device b // 16, devices numbered region-major. The live slots of one device name at most 16 buses owned by any one device of its own region and at most 8 buses owned in any one other region; in every draw every device reaches both bounds. A bus owned in another region is owned by the device with the same dev index there. `counts`: among the 8 areas of each device one has 16 live slots and the others at least 8. `factor`: unit lower triangular: ones on the diagonal, zeros above it. Rows below 64 of every area have inverse pivots of 0.10 or more; the other rows have them up to 0.14 as well.
All inputs are finite; a program needn't handle non-finite values.
Results may differ from a plain program's by a relative error of at most 0.005.
Values sent between devices are 32-bit elements; how exact they have to be, the bound alone decides.
A program may use at most 64 MiB of HBM per device.

v0:
```python
import functools

import jax
import jax.numpy as jnp
from jax import lax
from jax.experimental import pallas as pl
from jax.experimental.pallas import tpu as pltpu
from jax.sharding import PartitionSpec as P

ROWS_SLOT = 4
BLK = 128
BUS_DEV = 16
ITERS = 14
RHO = 4.0
SIGMA = 1.0
TILE = 256
F32 = jnp.float32
BF16 = jnp.bfloat16
MESH = pl.DeviceIdType.MESH
NT = (((1,), (1,)), ((), ()))
NN = (((1,), (0,)), ((), ()))


def mm(left, right, dims=NN):
    return lax.dot_general(left, right, dims, preferred_element_type=F32)


def split3(x):
    high = x.astype(BF16)
    rest = x - high.astype(F32)
    mid = rest.astype(BF16)
    low = (rest - mid.astype(F32)).astype(BF16)
    return high, mid, low


def kernel(
    n_region, n_dev, area_count, scenarios, order, slots,
    loads_hbm, factor_ref, pivots_hbm, lower_hbm, upper_hbm, row_ref, col_ref,
    dispatch_ref, duals_ref, res_ref,
    loads_ref, pivots_ref, lower_ref, upper_ref, fac, gram, diag, wide, edges, hot, known, known_b, diag_b, rounded, offset,
    pick, place, live, rhs_b, base_b, off_b, loads_b, low_b, up_b, blk, duals,
    part, got, table, mean, counts_got, members, res_sum, res_near, res_far,
    in_sem, fac_sem, send_sem, back_send, got_sem, table_sem, counts_sem, near_sem, far_sem,
):
    me_r = lax.axis_index("region")
    me_d = lax.axis_index("dev")
    items = area_count * slots
    rows = area_count * scenarios
    places = ROWS_SLOT * items
    edge = slots * ROWS_SLOT
    groups = n_dev + n_region
    near = [lax.rem(me_d + step, n_dev) for step in range(1, n_dev)]
    far = [lax.rem(me_r + step, n_region) for step in range(1, n_region)]
    peers = [((r, me_d), n_dev + r, n_dev + me_r, n_dev + r) for r in far]
    peers += [((me_r, d), d, me_d, d) for d in near]

    def factor_copy(area):
        return pltpu.make_async_copy(factor_ref.at[area], fac.at[area], fac_sem.at[area])

    inputs = [
        pltpu.make_async_copy(held, here, in_sem.at[number])
        for number, (held, here) in enumerate(
            ((loads_hbm, loads_ref), (pivots_hbm, pivots_ref), (lower_hbm, lower_ref), (upper_hbm, upper_ref))
        )
    ]
    for copy in inputs:
        copy.start()
    for area in range(area_count):
        factor_copy(area).start()

    got[...] = jnp.zeros_like(got)
    counts_got[...] = jnp.zeros_like(counts_got)
    table[...] = jnp.zeros_like(table)
    res_sum[...] = jnp.zeros_like(res_sum)

    barrier = pltpu.get_barrier_semaphore()
    for device, _, _, _ in peers:
        pl.semaphore_signal(barrier, inc=1, device_id=device, device_id_type=MESH)
    pl.semaphore_wait(barrier, len(peers))

    def group_rows(index):
        return pl.ds(pl.multiple_of(index * BUS_DEV, BUS_DEV), BUS_DEV)

    def outgoing(number, target, semaphores):
        device, theirs, mine, _ = peers[number]
        return pltpu.make_async_remote_copy(
            src_ref=part.at[group_rows(theirs)], dst_ref=target.at[group_rows(mine)],
            send_sem=send_sem.at[number], recv_sem=semaphores.at[mine],
            device_id=device, device_id_type=MESH,
        )

    def incoming(number, target, semaphores):
        device, theirs, _, here = peers[number]
        return pltpu.make_async_remote_copy(
            src_ref=part.at[group_rows(theirs)], dst_ref=target.at[group_rows(here)],
            send_sem=send_sem.at[number], recv_sem=semaphores.at[here],
            device_id=device, device_id_type=MESH,
        )

    def back(number, here=False):
        device, _, mine, theirs = peers[number]
        at = theirs if here else mine
        return pltpu.make_async_remote_copy(
            src_ref=mean, dst_ref=table.at[group_rows(at)],
            send_sem=back_send.at[number], recv_sem=table_sem.at[at],
            device_id=device, device_id_type=MESH,
        )

    def group_sum(ref):
        total = ref[0:BUS_DEV, :]
        for index in range(1, groups):
            total = total + ref[index * BUS_DEV : (index + 1) * BUS_DEV, :]
        return total

    picked = lax.broadcasted_iota(jnp.int32, (groups * BUS_DEV, items), 0) == row_ref[...]
    picked = jnp.where(picked, 1.0, 0.0)
    part[...] = jnp.broadcast_to(jnp.sum(picked, axis=1, keepdims=True), part.shape)
    for number in range(len(peers)):
        outgoing(number, counts_got, counts_sem).start()
    pick[...] = picked.astype(BF16)
    placed = lax.broadcasted_iota(jnp.int32, (items, groups * BUS_DEV), 1) == col_ref[...]
    place[...] = jnp.where(placed, 1.0, 0.0).astype(BF16)
    live[...] = jnp.broadcast_to(jnp.where(row_ref[...] >= 0, 1.0, 0.0), live.shape)
    counts_got[group_rows(me_d), :] = part[group_rows(me_d), :]

    def place_of(index):
        return lax.rem(index // slots, area_count), lax.rem(index, slots) * ROWS_SLOT + index // items

    source = lax.broadcasted_iota(jnp.int32, (area_count * BLK, places), 0)
    area_of, column_of = place_of(lax.broadcasted_iota(jnp.int32, (area_count * BLK, places), 1))
    hot[...] = jnp.where(source == area_of * BLK + column_of, 1.0, 0.0).astype(BF16)

    def stack_rows(x):
        return jnp.concatenate([x[:, r * items : (r + 1) * items] for r in range(ROWS_SLOT)], axis=0)

    def to_flat(x):
        parts = mm(jnp.concatenate(split3(x), axis=0), hot[...])
        return parts[:scenarios] + parts[scenarios : 2 * scenarios] + parts[2 * scenarios :]

    def line_flat(ref):
        line = jnp.concatenate([ref[a : a + 1, :BLK] for a in range(area_count)], axis=1)
        return to_flat(jnp.broadcast_to(line, (scenarios, area_count * BLK)))

    for copy in inputs:
        copy.wait()
    loads_b[...] = stack_rows(
        to_flat(jnp.concatenate([loads_ref[a, :, :BLK] for a in range(area_count)], axis=1))
    )
    low_b[...] = stack_rows(line_flat(lower_ref))
    up_b[...] = stack_rows(line_flat(upper_ref))

    tiles = order // TILE
    column = lax.broadcasted_iota(jnp.int32, (1, TILE), 1)
    cut = [slice(c * TILE, (c + 1) * TILE) for c in range(tiles)]

    for c in range(tiles):
        value = loads_ref[:, :, cut[c]].reshape(rows, TILE)
        if c == 0:
            value = jnp.where(column < edge, 0.0, value)
        rounded[:, cut[c]] = value.astype(BF16)

    same = lax.broadcasted_iota(jnp.int32, (BLK, BLK), 0) == lax.broadcasted_iota(jnp.int32, (BLK, BLK), 1)
    unit = jnp.where(same, 1.0, 0.0).astype(BF16)

    def product(area, carry):
        at = pl.ds(pl.multiple_of(area * scenarios, scenarios), scenarios)
        scaled = []
        for c in range(tiles):
            end = (c + 1) * TILE
            forward = mm(rounded[at, :end], fac[area, cut[c], :end], NT)
            scaled.append((forward * pivots_ref[pl.ds(area, 1), cut[c]]).astype(BF16))
        scaled = jnp.concatenate(scaled, axis=1)
        for c in range(tiles):
            known[at, cut[c]] = mm(scaled[:, c * TILE :], fac[area, c * TILE :, cut[c]])
        return carry

    def form(area, carry):
        factor_copy(area).wait()
        pivot = pivots_ref[pl.ds(area, 1), :]
        flipped = (mm(unit, fac[area, :, :BLK], NT) * pivot).astype(BF16)
        for n in range(tiles):
            value = mm(flipped[:, n * TILE :], fac[area, n * TILE :, cut[n]])
            if n == 0:
                head = value[:, :BLK]
                exact = pivot[:, :BLK]
                found = jnp.sum(jnp.where(same, head, 0.0), axis=0, keepdims=True)
                diag[pl.ds(area, 1), :] = found - exact.astype(BF16).astype(F32) + exact
                value = jnp.concatenate([jnp.where(same, 0.0, head), value[:, BLK:]], axis=1)
            gram[area, :, cut[n]] = value.astype(BF16)
        product(area, carry)
        return carry

    lax.fori_loop(0, area_count, form, 0)

    target = lax.broadcasted_iota(jnp.int32, (places, area_count * BLK), 1)
    area_of, column_of = place_of(lax.broadcasted_iota(jnp.int32, (places, area_count * BLK), 0))
    hot_rows = jnp.where(target == area_of * BLK + column_of, 1.0, 0.0).astype(BF16)
    for c in range(tiles):
        joined = jnp.concatenate([gram[a, :, cut[c]] for a in range(area_count)], axis=0)
        wide[:, cut[c]] = mm(hot_rows, joined).astype(BF16)
    source = lax.broadcasted_iota(jnp.int32, (BLK, places), 0)
    _, column_of = place_of(lax.broadcasted_iota(jnp.int32, (BLK, places), 1))
    spread = jnp.where(source == column_of, 1.0, 0.0).astype(BF16)
    area_left, _ = place_of(lax.broadcasted_iota(jnp.int32, (places, places), 0))
    area_right, _ = place_of(lax.broadcasted_iota(jnp.int32, (places, places), 1))
    edges[...] = jnp.where(area_left == area_right, mm(wide[:, :BLK], spread), 0.0).astype(BF16)
    diag_b[...] = line_flat(diag)

    offset[...] = jnp.zeros_like(offset)
    off_b[...] = jnp.zeros_like(off_b)
    duals[...] = jnp.zeros_like(duals)
    mean[...] = jnp.zeros_like(mean)
    rhs_b[...] = loads_b[...]

    for number in range(len(peers)):
        incoming(number, counts_got, counts_sem).wait_recv()
        outgoing(number, counts_got, counts_sem).wait_send()
    members[...] = jnp.maximum(group_sum(counts_got), 1.0)

    own_area, _ = place_of(lax.broadcasted_iota(jnp.int32, (scenarios, places), 1))

    def known_edges():
        joined = [known[a * scenarios : (a + 1) * scenarios, :BLK] for a in range(area_count)]
        known_b[...] = to_flat(jnp.concatenate(joined, axis=1))

    known_edges()

    _, column_of = place_of(lax.broadcasted_iota(jnp.int32, (places, BLK), 0))
    back_hot = lax.broadcasted_iota(jnp.int32, (places, BLK), 1) == column_of
    back_hot = jnp.where(back_hot, 1.0, 0.0).astype(BF16)

    def iterate(step, carry):
        turned = rhs_b[...]
        flat = jnp.concatenate(
            [turned[r * scenarios : (r + 1) * scenarios, :] for r in range(ROWS_SLOT)], axis=1
        )
        flat = flat.astype(BF16)
        solved = known_b[...] + mm(flat, edges[...]) + flat.astype(F32) * diag_b[...]
        block = stack_rows(solved)
        blk[...] = block
        values = (block + duals[...]) * live[...]
        pieces = split3(values)
        part[...] = mm(pick[...], pieces[0], NT) + mm(pick[...], pieces[1], NT) + mm(pick[...], pieces[2], NT)
        for number in range(len(peers)):
            outgoing(number, got, got_sem).start()
        got[group_rows(me_d), :] = part[group_rows(me_d), :]
        moved = block + off_b[...]
        boxed = jnp.clip(moved, low_b[...], up_b[...])
        rest = moved - boxed
        off_b[...] = rest
        base_b[...] = loads_b[...] + SIGMA * (boxed - rest)

        left = jnp.concatenate(
            [jnp.where(own_area == a, flat.astype(F32), 0.0) for a in range(area_count)], axis=0
        ).astype(BF16)
        for c in range(tiles):
            found = known[:, cut[c]] + mm(left, wide[:, cut[c]])
            found = found.reshape(area_count, scenarios, TILE)
            if c == 0:
                natural = mm(left, back_hot).reshape(area_count, scenarios, BLK) * diag[...][:, None, :]
                found = jnp.concatenate([found[:, :, :BLK] + natural, found[:, :, BLK:]], axis=2)
            dispatch_ref[:, :, cut[c]] = found
            moved = found + offset[:, :, cut[c]]
            boxed = jnp.clip(moved, lower_ref[:, cut[c]][:, None, :], upper_ref[:, cut[c]][:, None, :])
            rest = moved - boxed
            offset[:, :, cut[c]] = rest
            value = (loads_ref[:, :, cut[c]] + SIGMA * (boxed - rest)).reshape(rows, TILE)
            if c == 0:
                value = jnp.where(column < edge, 0.0, value)
            rounded[:, cut[c]] = value.astype(BF16)

        more = step < ITERS - 1

        @pl.when(more)
        def _():
            lax.fori_loop(0, area_count // 2, product, 0)

        for number in range(len(peers)):
            incoming(number, got, got_sem).wait_recv()
        fresh = group_sum(got) / members[...]
        change = fresh - mean[...]
        mean[...] = fresh
        for number in range(len(peers)):
            back(number).start()
        table[group_rows(me_d), :] = fresh
        res_sum[pl.ds(16 + step, 1), :] = (RHO * RHO) * jnp.sum(change * change, axis=0, keepdims=True)

        @pl.when(more)
        def _():
            lax.fori_loop(area_count // 2, area_count, product, 0)
            known_edges()

        for number in range(len(peers)):
            back(number, here=True).wait_recv()
        pieces = split3(table[...])
        z_slot = (mm(place[...], pieces[0]) + mm(place[...], pieces[1]) + mm(place[...], pieces[2])).T
        gap = (blk[...] - z_slot) * live[...]
        fresh_duals = duals[...] + gap
        duals[...] = fresh_duals
        rhs_b[...] = base_b[...] + RHO * (live[...] * (z_slot - fresh_duals))
        res_sum[pl.ds(step, 1), :] = jnp.sum(gap * gap, axis=0, keepdims=True)
        for number in range(len(peers)):
            outgoing(number, got, got_sem).wait_send()
            back(number).wait_send()
        return carry

    lax.fori_loop(0, ITERS, iterate, 0)

    def near_copy(number, here=False):
        device, _, mine, theirs = peers[number]
        at = theirs if here else mine
        return pltpu.make_async_remote_copy(
            src_ref=res_sum, dst_ref=res_near.at[at],
            send_sem=send_sem.at[number], recv_sem=near_sem.at[at], device_id=device, device_id_type=MESH,
        )

    def far_copy(number, here=False):
        device, _, mine, theirs = peers[number]
        at = (theirs if here else mine) - n_dev
        return pltpu.make_async_remote_copy(
            src_ref=res_sum, dst_ref=res_far.at[at],
            send_sem=send_sem.at[number], recv_sem=far_sem.at[at], device_id=device, device_id_type=MESH,
        )

    fars = range(n_region - 1)
    nears = range(n_region - 1, len(peers))
    for number in nears:
        near_copy(number).start()
    res_near[pl.ds(me_d, 1)] = res_sum[...][None]
    lane_from = lax.broadcasted_iota(jnp.int32, (BLK, BLK), 0)
    lane_to = lax.broadcasted_iota(jnp.int32, (BLK, BLK), 1)
    wanted = lax.rem(lane_to, ROWS_SLOT) * scenarios + lane_to // ROWS_SLOT
    lanes_hot = jnp.where(lane_from == wanted, 1.0, 0.0).astype(BF16)
    pieces = split3(duals[...].T)
    duals_ref[...] = mm(pieces[0], lanes_hot) + mm(pieces[1], lanes_hot) + mm(pieces[2], lanes_hot)
    for number in nears:
        near_copy(number, here=True).wait_recv()
        near_copy(number).wait_send()
    total = res_near[0]
    for index in range(1, n_dev):
        total = total + res_near[index]
    res_sum[...] = total
    for number in fars:
        far_copy(number).start()
    res_far[pl.ds(me_r, 1)] = total[None]
    for number in fars:
        far_copy(number, here=True).wait_recv()
        far_copy(number).wait_send()
    total = res_far[0]
    for index in range(1, n_region):
        total = total + res_far[index]
    sums = jnp.sum(total, axis=1, keepdims=True) / float(area_count * n_dev * n_region * BLK)
    lane = lax.broadcasted_iota(jnp.int32, (16, BLK), 1)
    res_ref[...] = jnp.where(lane == 0, sums[:16], sums[16:])


def on_device(loads, factor, pivots, lower, upper, incidence, counts):
    area_count, scenarios, order = loads.shape
    slots = incidence.shape[1]
    items = area_count * slots
    n_dev = lax.axis_size("dev")
    n_region = lax.axis_size("region")
    groups = n_dev + n_region
    peers = groups - 2
    table_rows = groups * BUS_DEV
    places = ROWS_SLOT * items
    rows = area_count * scenarios
    live_slot = jnp.arange(slots)[None, :] < counts[:, None]
    owner = incidence // BUS_DEV
    near = owner // n_dev == lax.axis_index("region")
    group = jnp.where(near, owner % n_dev, n_dev + owner // n_dev)
    at = jnp.where(live_slot, group * BUS_DEV + incidence % BUS_DEV, -1).astype(jnp.int32)

    vmem = pl.BlockSpec(memory_space=pltpu.VMEM)
    square = pltpu.VMEM((items, BLK), F32)
    bus = pltpu.VMEM((BUS_DEV, BLK), F32)
    listed = pltpu.VMEM((table_rows, BLK), F32)
    dma = pltpu.SemaphoreType.DMA
    dispatch, duals, res = pl.pallas_call(
        functools.partial(kernel, n_region, n_dev, area_count, scenarios, order, slots),
        out_shape=(
            jax.ShapeDtypeStruct(loads.shape, F32),
            jax.ShapeDtypeStruct((items, BLK), F32),
            jax.ShapeDtypeStruct((16, BLK), F32),
        ),
        in_specs=[pl.BlockSpec(memory_space=pltpu.HBM)] * 5 + [vmem] * 2,
        out_specs=(vmem, vmem, vmem),
        scratch_shapes=[
            pltpu.VMEM(loads.shape, F32),
            pltpu.VMEM(pivots.shape, F32),
            pltpu.VMEM(lower.shape, F32),
            pltpu.VMEM(upper.shape, F32),
            pltpu.VMEM((area_count, order, order), BF16),
            pltpu.VMEM((area_count, BLK, order), BF16),
            pltpu.VMEM((area_count, BLK), F32),
            pltpu.VMEM((places, order), BF16),
            pltpu.VMEM((places, places), BF16),
            pltpu.VMEM((area_count * BLK, places), BF16),
            pltpu.VMEM((rows, order), F32),
            pltpu.VMEM((scenarios, places), F32),
            pltpu.VMEM((scenarios, places), F32),
            pltpu.VMEM((rows, order), BF16),
            pltpu.VMEM(loads.shape, F32),
            pltpu.VMEM((table_rows, items), BF16),
            pltpu.VMEM((items, table_rows), BF16),
            square, square, square, square, square, square, square, square, square,
            listed, listed, listed, bus, listed, bus,
            pltpu.VMEM((32, BLK), F32),
            pltpu.VMEM((n_dev, 32, BLK), F32),
            pltpu.VMEM((n_region, 32, BLK), F32),
            dma((4,)), dma((area_count,)), dma((peers,)), dma((peers,)), dma((groups,)), dma((groups,)), dma((groups,)),
            dma((n_dev,)), dma((n_region,)),
        ],
        compiler_params=pltpu.CompilerParams(
            collective_id=0, has_side_effects=True, vmem_limit_bytes=48 * 1024 * 1024
        ),
        name="admm",
    )(loads, factor, pivots, lower, upper, at.reshape(1, items), at.reshape(items, 1))
    return dispatch, duals.reshape(area_count, slots, BLK), res[:ITERS, :2]


def solution(mesh):
    placed = (
        P(("region", "dev"), None, None),
        P(("region", "dev"), None, None),
        P(("region", "dev"), None),
        P(("region", "dev"), None),
        P(("region", "dev"), None),
        P(("region", "dev"), None),
        P(("region", "dev")),
    )
    return jax.shard_map(
        on_device,
        mesh=mesh,
        in_specs=placed,
        out_specs=(P(("region", "dev"), None, None), P(("region", "dev"), None, None), P()),
        check_vma=False,
    )
```

profile of v0, /device:TPU:0, one launch (start us, length us, event | category | flops | bytes accessed | tf_op | source)
XLA Modules:
  0.0 150.3 jit_solution(15939083473172907275)
XLA Ops:
  0.6 0.8 fusion.3
  1.4 0.1 reshape.16.row_ref
  1.5 0.1 reshape.19.col_ref
  1.6 0.0 copy-start
  1.6 1.2 copy-done
  2.8 0.0 copy-start.1
  2.8 0.8 copy-done.1
  3.6 0.0 copy-start.2
  3.6 0.8 copy-done.2
  4.3 0.0 copy-start.3
  4.3 0.8 copy-done.3
  5.1 143.0 %admm.1 = (f32[8,32,1024]{2,1,0:T(8,128)S(1)}, f32[128,128]{1,0:T(8,128)S(1)}, f32[16,128]{1,0:T(8,128)S(1)}) custom-call(f32[8,32,1024]{2,1,0:T(8,128)S(1)} %copy-done, bf16[8,1024,1024]{2,1,0:T(8,128)(2,1)} %factor_ref.1, f32[8,1024]{1,0:T(8,128)S(1)} %copy-done.1, f32[8,1024]{1,0:T(8,128)S(1)} %copy-done.2, f32[8,1024]{1,0:T(8,128)S(1)} %copy-done.3, ...), custom_call_target="tpu_custom_call" | custom-call | tf_op jit(solution)/shard_map/admm/pallas_call | solution.py:379
  148.1 0.6 copy.11
  148.7 1.0 copy.14
  149.7 0.6 copy.15
Async XLA Ops:
  1.6 1.2 copy-start
  2.8 0.8 copy-start.1
  3.6 0.8 copy-start.2
  4.3 0.8 copy-start.3
where the time goes:
time: 151 us; the launch traced here: 150 us
  Pallas kernels  143 us (95%)
  local copies, waits for them, and re-layouts  5.9 us (4%)
    pallas_call x1, Pallas kernels, on_device(): pl.pallas_call(functools.partial(kernel, n_region, n_dev, area_count, sce...  143 us
    unnamed x11, local copies, waits for them, and re-layouts  5.74 us

commit v1 on v0

--- a/solution.py
+++ b/solution.py
@@ -162,16 +162,25 @@
     same = lax.broadcasted_iota(jnp.int32, (BLK, BLK), 0) == lax.broadcasted_iota(jnp.int32, (BLK, BLK), 1)
     unit = jnp.where(same, 1.0, 0.0).astype(BF16)
 
-    def product(area, carry):
+    def forward_of(area):
         at = pl.ds(pl.multiple_of(area * scenarios, scenarios), scenarios)
         scaled = []
         for c in range(tiles):
             end = (c + 1) * TILE
             forward = mm(rounded[at, :end], fac[area, cut[c], :end], NT)
             scaled.append((forward * pivots_ref[pl.ds(area, 1), cut[c]]).astype(BF16))
-        scaled = jnp.concatenate(scaled, axis=1)
+        return jnp.concatenate(scaled, axis=1)
+
+    def back_of(area, scaled):
+        at = pl.ds(pl.multiple_of(area * scenarios, scenarios), scenarios)
         for c in range(tiles):
             known[at, cut[c]] = mm(scaled[:, c * TILE :], fac[area, c * TILE :, cut[c]])
+
+    def product(pair, carry):
+        first = forward_of(2 * pair)
+        second = forward_of(2 * pair + 1)
+        back_of(2 * pair, first)
+        back_of(2 * pair + 1, second)
         return carry
 
     def form(area, carry):
@@ -187,7 +196,7 @@
                 diag[pl.ds(area, 1), :] = found - exact.astype(BF16).astype(F32) + exact
                 value = jnp.concatenate([jnp.where(same, 0.0, head), value[:, BLK:]], axis=1)
             gram[area, :, cut[n]] = value.astype(BF16)
-        product(area, carry)
+        back_of(area, forward_of(area))
         return carry
 
     lax.fori_loop(0, area_count, form, 0)
@@ -221,7 +230,11 @@
 
     def known_edges():
         joined = [known[a * scenarios : (a + 1) * scenarios, :BLK] for a in range(area_count)]
-        known_b[...] = to_flat(jnp.concatenate(joined, axis=1))
+        joined = jnp.concatenate(joined, axis=1)
+        high = joined.astype(BF16)
+        low = (joined - high.astype(F32)).astype(BF16)
+        parts = mm(jnp.concatenate([high, low], axis=0), hot[...])
+        known_b[...] = parts[:scenarios] + parts[scenarios:]
 
     known_edges()
 
@@ -256,9 +269,6 @@
         for c in range(tiles):
             found = known[:, cut[c]] + mm(left, wide[:, cut[c]])
             found = found.reshape(area_count, scenarios, TILE)
-            if c == 0:
-                natural = mm(left, back_hot).reshape(area_count, scenarios, BLK) * diag[...][:, None, :]
-                found = jnp.concatenate([found[:, :, :BLK] + natural, found[:, :, BLK:]], axis=2)
             dispatch_ref[:, :, cut[c]] = found
             moved = found + offset[:, :, cut[c]]
             boxed = jnp.clip(moved, lower_ref[:, cut[c]][:, None, :], upper_ref[:, cut[c]][:, None, :])
@@ -271,9 +281,14 @@
 
         more = step < ITERS - 1
 
+        @pl.when(step == ITERS - 1)
+        def _():
+            natural = mm(left, back_hot).reshape(area_count, scenarios, BLK) * diag[...][:, None, :]
+            dispatch_ref[:, :, :BLK] = dispatch_ref[:, :, :BLK] + natural
+
         @pl.when(more)
         def _():
-            lax.fori_loop(0, area_count // 2, product, 0)
+            lax.fori_loop(0, area_count // 4, product, 0)
 
         for number in range(len(peers)):
             incoming(number, got, got_sem).wait_recv()
@@ -287,7 +302,7 @@
 
         @pl.when(more)
         def _():
-            lax.fori_loop(area_count // 2, area_count, product, 0)
+            lax.fori_loop(area_count // 4, area_count // 2, product, 0)
             known_edges()
 
         for number in range(len(peers)):

time: 151 us -> 147 us (0.974)
  Pallas kernels: 143 us -> 139 us
    pallas_call x1, Pallas kernels: 143 us -> 139 us  [on_device(): pl.pallas_call(functools.partial(kernel, n_region, n_dev, area_count, sce...]
where the time goes in v1:
time: 147 us; the launch traced here: 146 us
  Pallas kernels  139 us (95%)
  local copies, waits for them, and re-layouts  5.9 us (4%)
    pallas_call x1, Pallas kernels, on_device(): pl.pallas_call(functools.partial(kernel, n_region, n_dev, area_count, sce...  139 us
    unnamed x11, local copies, waits for them, and re-layouts  5.74 us

profile of v1, /device:TPU:0, one launch (start us, length us, event | category | flops | bytes accessed | tf_op | source)
XLA Modules:
  0.0 146.2 jit_solution(10255152071941506069)
XLA Ops:
  0.6 0.8 fusion.3
  1.4 0.1 reshape.16.row_ref
  1.5 0.1 reshape.19.col_ref
  1.6 0.0 copy-start
  1.6 1.2 copy-done
  2.8 0.0 copy-start.1
  2.8 0.8 copy-done.1
  3.6 0.0 copy-start.2
  3.6 0.8 copy-done.2
  4.3 0.0 copy-start.3
  4.3 0.8 copy-done.3
  5.1 138.9 %admm.1 = (f32[8,32,1024]{2,1,0:T(8,128)S(1)}, f32[128,128]{1,0:T(8,128)S(1)}, f32[16,128]{1,0:T(8,128)S(1)}) custom-call(f32[8,32,1024]{2,1,0:T(8,128)S(1)} %copy-done, bf16[8,1024,1024]{2,1,0:T(8,128)(2,1)} %factor_ref.1, f32[8,1024]{1,0:T(8,128)S(1)} %copy-done.1, f32[8,1024]{1,0:T(8,128)S(1)} %copy-done.2, f32[8,1024]{1,0:T(8,128)S(1)} %copy-done.3, ...), custom_call_target="tpu_custom_call" | custom-call | tf_op jit(solution)/shard_map/admm/pallas_call | solution.py:394
  144.0 0.6 copy.11
  144.6 1.0 copy.14
  145.6 0.6 copy.15
Async XLA Ops:
  1.6 1.2 copy-start
  2.8 0.8 copy-start.1
  3.6 0.8 copy-start.2
  4.3 0.8 copy-start.3
